TPU v7x, 32 devices: a whole 2x2x4 slice. The times are simulated.
32 devices in a mesh: row: 8 (over y, x, core), col: 4 (over z).
Axes of the slice: x: 2, y: 2, z: 4, core: 2. Of those that a mesh axis runs over, the one named last changes fastest.
Arguments:
- q_child: float32 [16384, 32768], P('row', 'col'), may hold values from -6 to 6
- sec_weights: float32 [65536, 256], P(('row', 'col')), may hold values from -3000 to 3000
- deflated: int32 [65536], P(('row', 'col')), may hold values 0 or 1
- local_perm: int32 [32, 2048], P(('row', 'col')), may hold values from 0 to 2047, each once within a row
- owner_order: int32 [2, 4], replicated, may hold values from 0 to 3, each once within a row
Outputs:
- merged: float32 [16384, 256], P(('row', 'col'))
Inputs may be any that keep to these rules, and one draw needn't show every extreme that they name: `local_perm`: each row is a permutation of 0 to 2047. `owner_order`: each row is a permutation of 0 to 3.
All inputs are finite; a program needn't handle non-finite values. No bound on the sum of `deflated` on one device may be relied on, other than what follows from the above.
Results may differ from a plain program's by a relative error of at most 0.000073.
Values sent between devices are 32-bit elements; how exact they have to be, the bound alone decides.
A program may use at most 192 MiB of HBM per device.

v0:
```python
import jax
import jax.numpy as jnp
from jax import lax
from jax.sharding import PartitionSpec as P


def passed_along(array, axis, by):
    length = lax.axis_size(axis)
    return lax.ppermute(array, axis, [(i, (i + by) % length) for i in range(length)])


def shifted(array, axis, by):
    length = lax.axis_size(axis)
    pairs = [(i, i + by) for i in range(length) if 0 <= i + by < length]
    return lax.ppermute(array, axis, pairs)


def per_device(q_child, sec_weights, deflated, local_perm, owner_order):
    kept_rows = (1 - deflated).astype(jnp.float32)[:, None]
    masked = sec_weights * kept_rows
    col_total = lax.psum(jnp.sum(masked * masked, axis=0), ("row", "col"))
    scaled = masked * lax.rsqrt(col_total + 1e-06)[None, :]
    ordered = jnp.take(scaled, local_perm[0], axis=0)
    piece_rows = ordered.shape[0]
    row_count = lax.axis_size("row")
    col_count = lax.axis_size("col")
    half_count = row_count // 2
    row_index = lax.axis_index("row")
    col_index = lax.axis_index("col")
    child_half = row_index // half_count
    place_in_half = row_index % half_count
    targets = lax.dynamic_index_in_dim(owner_order, child_half, 0, keepdims=False)

    def advance(shifts, carry):
        travel, holding = carry
        travel = passed_along(travel, "col", 1)
        source = (col_index - shifts) % col_count
        holding = jnp.where(targets[source] == col_index, travel, holding)
        return (travel, holding)

    start_hold = jnp.where(targets[col_index] == col_index, ordered, jnp.zeros_like(ordered))
    _, holding = lax.fori_loop(1, col_count, advance, (ordered, start_hold))
    empty_block = jnp.zeros((half_count * piece_rows, holding.shape[1]), holding.dtype)
    own_block = lax.dynamic_update_slice_in_dim(empty_block, holding, place_in_half * piece_rows, 0)

    def collect_step(steps, carry):
        going_up, going_down, block = carry
        going_up = shifted(going_up, "row", 1)
        going_down = shifted(going_down, "row", -1)
        below = place_in_half - steps
        above = place_in_half + steps
        below_slot = jnp.clip(below, 0, half_count - 1)
        above_slot = jnp.clip(above, 0, half_count - 1)
        with_below = lax.dynamic_update_slice_in_dim(block, going_up, below_slot * piece_rows, 0)
        block = jnp.where(below >= 0, with_below, block)
        with_above = lax.dynamic_update_slice_in_dim(block, going_down, above_slot * piece_rows, 0)
        block = jnp.where(above < half_count, with_above, block)
        return (going_up, going_down, block)

    _, _, secular_block = lax.fori_loop(1, half_count, collect_step, (holding, holding, own_block))
    return lax.psum_scatter(
        jnp.dot(
            q_child,
            secular_block,
            precision=lax.Precision.HIGHEST,
            preferred_element_type=jnp.float32,
        ),
        "col",
        scatter_dimension=0,
        tiled=True,
    )


def solution(mesh):
    placed = (
        P("row", "col"),
        P(("row", "col"), None),
        P(("row", "col")),
        P(("row", "col"), None),
        P(),
    )
    return jax.shard_map(
        per_device, mesh=mesh, in_specs=placed, out_specs=P(("row", "col"), None), check_vma=False
    )
```

profile of v0, /device:TPU:0, one launch (start us, length us, event | category | flops | bytes accessed | tf_op | source)
XLA Modules:
  0.0 570.6 jit_solution(5938329069474959783)
XLA Ops:
  9.7 1.9 multiply_reduce_fusion
  11.7 42.0 %psum.7 = f32[256]{0:T(256)S(1)} all-reduce(f32[256]{0:T(256)S(1)} %multiply_reduce_fusion), channel_id=1, replica_groups=mesh['row'=8,'col'=4] {'row','col'}, use_global_device_ids=true, to_apply=%region_1.0 | all-reduce | flops 256 | bytes 2048 | tf_op jit(solution)/shard_map/psum | solution.py:21
  53.7 1.9 multiply_multiply_fusion
  55.7 8.6 %gather_fusion = f32[2048,256]{1,0:T(8,128)} fusion(f32[2048,256]{1,0:T(8,128)S(1)} %multiply_multiply_fusion, s32[2048]{0:T(1024)S(1)} %broadcast_clamp_fusion), kind=kCustom, calls=%fused_computation | custom fusion | bytes 4202496 | tf_op jit(solution)/shard_map/jit(_take)/gather | solution.py:23
  64.3 3.4 broadcast_select_fusion.1
  67.7 152.2 %while.34 = (s32[]{:T(128)}, f32[2048,256]{1,0:T(8,128)}, f32[2048,256]{1,0:T(8,128)}, s32[]{:T(128)}, s32[4]{0:T(128)S(1)}, /*index=5*/s32[]{:T(128)}, s32[]{:T(128)}, s32[]{:T(128)}, s32[]{:T(128)}) while((s32[]{:T(128)}, f32[2048,256]{1,0:T(8,128)}, f32[2048,256]{1,0:T(8,128)}, s32[]{:T(128)}, s32[4]{0:T(128)S(1)}, /*index=5*/s32[]{:T(128)}, ...), condition=%wide.region_3.4_spmd, body=%wide.region_2.3_spmd.sunk | while | flops 524306 | bytes 35651940 | solution.py:42
  67.7 1.5 collective-permute-start
  70.5 45.7 %collective-permute-done = f32[2048,256]{1,0:T(8,128)S(1)} collective-permute-done((f32[2048,256]{1,0:T(8,128)}, f32[2048,256]{1,0:T(8,128)S(1)}, u32[]{:S(2)}, u32[]{:S(2)}) %collective-permute-start) | collective-permute-done | bytes 2097184 | tf_op jit(solution)/shard_map/while/body/eval_jaxpr/ppermute | solution.py:9
  120.7 46.3 %collective-permute-done = f32[2048,256]{1,0:T(8,128)S(1)} collective-permute-done((f32[2048,256]{1,0:T(8,128)}, f32[2048,256]{1,0:T(8,128)S(1)}, u32[]{:S(2)}, u32[]{:S(2)}) %collective-permute-start) | collective-permute-done | bytes 2097184 | tf_op jit(solution)/shard_map/while/body/eval_jaxpr/ppermute | solution.py:9
  171.4 45.4 %collective-permute-done = f32[2048,256]{1,0:T(8,128)S(1)} collective-permute-done((f32[2048,256]{1,0:T(8,128)}, f32[2048,256]{1,0:T(8,128)S(1)}, u32[]{:S(2)}, u32[]{:S(2)}) %collective-permute-start) | collective-permute-done | bytes 2097184 | tf_op jit(solution)/shard_map/while/body/eval_jaxpr/ppermute | solution.py:9
  219.9 3.1 copy.22
  224.7 3.2 copy-done
  227.9 135.3 %while.35 = (s32[]{:T(128)}, f32[2048,256]{1,0:T(8,128)}, f32[2048,256]{1,0:T(8,128)}, f32[8192,256]{1,0:T(8,128)}, s32[]{:T(128)}, /*index=5*/s32[]{:T(128)}, s...) while((s32[]{:T(128)}, f32[2048,256]{1,0:T(8,128)}, f32[2048,256]{1,0:T(8,128)}, ...), condition=%wide.region_5.6_spmd, body=%wide.region_4.5_spmd.sunk | while | flops 1048594 | bytes 104858024 | solution.py:60
  227.9 1.4 collective-permute-start.1
  230.7 2.5 collective-permute-done.1
  235.7 3.6 copy.30
  239.8 2.0 select_dynamic-update-slice_fusion.5
  241.8 3.2 copy-done.2
  245.0 42.5 %collective-permute-start.1 = (f32[2048,256]{1,0:T(8,128)}, f32[2048,256]{1,0:T(8,128)S(1)}, u32[]{:S(2)}, u32[]{:S(2)}) collective-permute-start(f32[2048,256]{1,0:T(8,128)} %get-tuple-element.357), channel_id=1, source_target_pairs={{0,4},{4,8},{8,12},{12,16},{16,20},{20,24},{24,28},{1,5},{5,9},{9,... | collective-permute-start | bytes 6291464 | tf_op jit(solution)/shard_map/while/body/eval_jaxpr/ppermute | solution.py:15
  288.9 2.5 collective-permute-done.1
  291.4 1.4 copy.29
  293.9 3.6 copy.30
  298.0 2.0 select_dynamic-update-slice_fusion.5
  300.0 3.2 copy-done.2
  303.3 44.2 %collective-permute-start.1 = (f32[2048,256]{1,0:T(8,128)}, f32[2048,256]{1,0:T(8,128)S(1)}, u32[]{:S(2)}, u32[]{:S(2)}) collective-permute-start(f32[2048,256]{1,0:T(8,128)} %get-tuple-element.357), channel_id=1, source_target_pairs={{0,4},{4,8},{8,12},{12,16},{16,20},{20,24},{24,28},{1,5},{5,9},{9,... | collective-permute-start | bytes 6291464 | tf_op jit(solution)/shard_map/while/body/eval_jaxpr/ppermute | solution.py:15
  348.8 2.5 collective-permute-done.1
  353.9 3.6 copy.30
  358.0 2.0 select_dynamic-update-slice_fusion.5
  360.0 3.2 copy-done.2
  363.2 112.1 %convolution_bitcast_fusion = f32[2048,256]{0,1:T(8,128)} fusion(f32[8192,256]{1,0:T(8,128)} %get-tuple-element.233, f32[2048,8192]{1,0:T(8,128)} %param.9), kind=kOutput, calls=%fused_computation.4 | convolution fusion | flops 51539607552 | bytes 77594624 | tf_op jit(solution)/shard_map/dot_general | solution.py:62
  475.4 86.4 %reduce-scatter.2.cloned.1.call-done = f32[512,256]{0,1:T(8,128)} async-done(((f32[2048,256]{0,1:T(8,128)}), f32[512,256]{0,1:T(8,128)}) %reduce-scatter.2.cloned.1.call-update) | async-done | bytes 524304 | tf_op jit(solution)/shard_map/reduce_scatter | solution.py:61
  561.7 2.0 copy.7
  (59 shorter events, 27.0 us)
Async XLA Ops:
  6.5 555.2 %reduce-scatter.2.cloned.1.call-start = ((), (), s32[]{:S(2)}) async-start(), calls=%async_computation.1 | async-start | bytes 2621440 | tf_op jit(solution)/shard_map/reduce_scatter | solution.py:61
  53.7 2.0 copy-start.6
  67.7 48.6 %collective-permute-start = (f32[2048,256]{1,0:T(8,128)}, f32[2048,256]{1,0:T(8,128)S(1)}, u32[]{:S(2)}, u32[]{:S(2)}) collective-permute-start(f32[2048,256]{1,0:T(8,128)} %get-tuple-element.328), channel_id=1, source_target_pairs={{0,1},{1,2},{2,3},{3,0},{4,5},{5,6},{6,7},{7,4},{8,9},{9,10},{10,1... | collective-permute-start | bytes 6291464 | tf_op jit(solution)/shard_map/while/body/eval_jaxpr/ppermute | solution.py:9
  70.5 47.1 %copy-start.3 = (f32[2048,256]{1,0:T(8,128)S(1)}, f32[2048,256]{1,0:T(8,128)}, u32[]{:S(2)}) copy-start(f32[2048,256]{1,0:T(8,128)} %get-tuple-element.329) | copy-start | bytes 6291460 | tf_op jit(solution)/shard_map/while
  118.0 1.4 copy-start.4
  119.3 47.6 %collective-permute-start = (f32[2048,256]{1,0:T(8,128)}, f32[2048,256]{1,0:T(8,128)S(1)}, u32[]{:S(2)}, u32[]{:S(2)}) collective-permute-start(f32[2048,256]{1,0:T(8,128)} %get-tuple-element.328), channel_id=1, source_target_pairs={{0,1},{1,2},{2,3},{3,0},{4,5},{5,6},{6,7},{7,4},{8,9},{9,10},{10,1... | collective-permute-start | bytes 6291464 | tf_op jit(solution)/shard_map/while/body/eval_jaxpr/ppermute | solution.py:9
  120.7 47.7 %copy-start.3 = (f32[2048,256]{1,0:T(8,128)S(1)}, f32[2048,256]{1,0:T(8,128)}, u32[]{:S(2)}) copy-start(f32[2048,256]{1,0:T(8,128)} %get-tuple-element.329) | copy-start | bytes 6291460 | tf_op jit(solution)/shard_map/while
  168.7 1.4 copy-start.4
  170.1 46.7 %collective-permute-start = (f32[2048,256]{1,0:T(8,128)}, f32[2048,256]{1,0:T(8,128)S(1)}, u32[]{:S(2)}, u32[]{:S(2)}) collective-permute-start(f32[2048,256]{1,0:T(8,128)} %get-tuple-element.328), channel_id=1, source_target_pairs={{0,1},{1,2},{2,3},{3,0},{4,5},{5,6},{6,7},{7,4},{8,9},{9,10},{10,1... | collective-permute-start | bytes 6291464 | tf_op jit(solution)/shard_map/while/body/eval_jaxpr/ppermute | solution.py:9
  171.4 46.7 %copy-start.3 = (f32[2048,256]{1,0:T(8,128)S(1)}, f32[2048,256]{1,0:T(8,128)}, u32[]{:S(2)}) copy-start(f32[2048,256]{1,0:T(8,128)} %get-tuple-element.329) | copy-start | bytes 6291460 | tf_op jit(solution)/shard_map/while
  218.5 1.4 copy-start.4
  222.9 1.6 copy-start.5
  224.7 3.2 copy-start
  227.9 5.3 collective-permute-start.1
  229.3 6.4 %collective-permute-start.2 = (f32[2048,256]{1,0:T(8,128)}, f32[2048,256]{1,0:T(8,128)}, u32[]{:S(2)}, u32[]{:S(2)}) collective-permute-start(f32[2048,256]{1,0:T(8,128)} %get-tuple-element.358), channel_id=1, source_target_pairs={{4,0},{8,4},{12,8},{16,12},{20,16},{24,20},{28,24},{5,1},{9,5},{13... | collective-permute-start | bytes 6291464 | tf_op jit(solution)/shard_map/while/body/eval_jaxpr/ppermute | solution.py:15
  233.2 6.2 %copy-start.1 = (f32[8192,256]{1,0:T(8,128)S(1)}, f32[8192,256]{1,0:T(8,128)}, u32[]{:S(2)}) copy-start(f32[8192,256]{1,0:T(8,128)} %get-tuple-element.359) | copy-start | bytes 25165828 | tf_op jit(solution)/shard_map/while
  241.8 3.2 copy-start.2
  245.0 46.3 %collective-permute-start.1 = (f32[2048,256]{1,0:T(8,128)}, f32[2048,256]{1,0:T(8,128)S(1)}, u32[]{:S(2)}, u32[]{:S(2)}) collective-permute-start(f32[2048,256]{1,0:T(8,128)} %get-tuple-element.357), channel_id=1, source_target_pairs={{0,4},{4,8},{8,12},{12,16},{16,20},{20,24},{24,28},{1,5},{5,9},{9,... | collective-permute-start | bytes 6291464 | tf_op jit(solution)/shard_map/while/body/eval_jaxpr/ppermute | solution.py:15
  287.5 6.4 %collective-permute-start.2 = (f32[2048,256]{1,0:T(8,128)}, f32[2048,256]{1,0:T(8,128)}, u32[]{:S(2)}, u32[]{:S(2)}) collective-permute-start(f32[2048,256]{1,0:T(8,128)} %get-tuple-element.358), channel_id=1, source_target_pairs={{4,0},{8,4},{12,8},{16,12},{20,16},{24,20},{28,24},{5,1},{9,5},{13... | collective-permute-start | bytes 6291464 | tf_op jit(solution)/shard_map/while/body/eval_jaxpr/ppermute | solution.py:15
  291.4 6.2 %copy-start.1 = (f32[8192,256]{1,0:T(8,128)S(1)}, f32[8192,256]{1,0:T(8,128)}, u32[]{:S(2)}) copy-start(f32[8192,256]{1,0:T(8,128)} %get-tuple-element.359) | copy-start | bytes 25165828 | tf_op jit(solution)/shard_map/while
  300.0 3.2 copy-start.2
  303.3 48.1 %collective-permute-start.1 = (f32[2048,256]{1,0:T(8,128)}, f32[2048,256]{1,0:T(8,128)S(1)}, u32[]{:S(2)}, u32[]{:S(2)}) collective-permute-start(f32[2048,256]{1,0:T(8,128)} %get-tuple-element.357), channel_id=1, source_target_pairs={{0,4},{4,8},{8,12},{12,16},{16,20},{20,24},{24,28},{1,5},{5,9},{9,... | collective-permute-start | bytes 6291464 | tf_op jit(solution)/shard_map/while/body/eval_jaxpr/ppermute | solution.py:15
  347.5 6.4 %collective-permute-start.2 = (f32[2048,256]{1,0:T(8,128)}, f32[2048,256]{1,0:T(8,128)}, u32[]{:S(2)}, u32[]{:S(2)}) collective-permute-start(f32[2048,256]{1,0:T(8,128)} %get-tuple-element.358), channel_id=1, source_target_pairs={{4,0},{8,4},{12,8},{16,12},{20,16},{24,20},{28,24},{5,1},{9,5},{13... | collective-permute-start | bytes 6291464 | tf_op jit(solution)/shard_map/while/body/eval_jaxpr/ppermute | solution.py:15
  351.3 6.2 %copy-start.1 = (f32[8192,256]{1,0:T(8,128)S(1)}, f32[8192,256]{1,0:T(8,128)}, u32[]{:S(2)}) copy-start(f32[8192,256]{1,0:T(8,128)} %get-tuple-element.359) | copy-start | bytes 25165828 | tf_op jit(solution)/shard_map/while
  360.0 3.2 copy-start.2
Sparse Core Ops, SparseCore 0:
  475.5 86.2 reduce-scatter.1
where the time goes:
time: 571 us
  waiting for transfers between devices  235 us (41%)
  matrix products  112 us (20%)
  starting transfers between devices  93.5 us (16%)
  local copies, waits for them, and re-layouts  55.3 us (10%)
  blocking collectives  42 us (7%)
  other arithmetic  16.4 us (3%)
  between operations  14 us (2%)
    ppermute x3, waiting for transfers between devices, passed_along(): lax.ppermute(array, axis, [(i, (i + by) % length) for i in range(length)])  137 us
    dot_general x1, matrix products, per_device(): jnp.dot(q_child, secular_block, precision=lax.Precision.HIGHEST, preferre...  112 us
    ppermute x6, starting transfers between devices, shifted(): return lax.ppermute(array, axis, pairs)  92 us
    reduce_scatter x1, waiting for transfers between devices, per_device(): lax.psum_scatter(jnp.dot(q_child, secular_block, precision=lax.Precision....  86.4 us
    psum x1, blocking collectives, per_device(): col_total = lax.psum(jnp.sum(masked * masked, axis=0), ('row', 'col'))  42 us
    while x33, local copies, waits for them, and re-layouts  32.8 us
  transfers between devices with their start and end apart: 10, of which 10 were waited for; matrix products, arithmetic and copies ran while one was open for 1% of the time, Pallas kernels for 0%

commit v1 on v0

--- a/solution.py
+++ b/solution.py
@@ -1,7 +1,13 @@
+import functools
 import jax
 import jax.numpy as jnp
 from jax import lax
+from jax.experimental import pallas as pl
+from jax.experimental.pallas import tpu as pltpu
 from jax.sharding import PartitionSpec as P
+
+CHUNKS = 8
+EDGE_IN, INNER_OWN, INNER_FORWARD, EDGE_OUT, TO_CORE, TO_X, DIAGONAL = range(7)
 
 
 def passed_along(array, axis, by):
@@ -15,21 +21,242 @@
     return lax.ppermute(array, axis, pairs)
 
 
-def per_device(q_child, sec_weights, deflated, local_perm, owner_order):
-    kept_rows = (1 - deflated).astype(jnp.float32)[:, None]
-    masked = sec_weights * kept_rows
-    col_total = lax.psum(jnp.sum(masked * masked, axis=0), ("row", "col"))
-    scaled = masked * lax.rsqrt(col_total + 1e-06)[None, :]
-    ordered = jnp.take(scaled, local_perm[0], axis=0)
+def merge_kernel(chunks, sel_ref, own_ref, q_ref, out_ref, zone, picked, blocks, acc, parts, q_tiles,
+                 send_sem, recv_sem, part_send, part_recv, q_sem):
+    piece, cols = own_ref.shape
+    size = piece // chunks
+    out_rows = out_ref.shape[0]
+    row = lax.axis_index("row")
+    col = lax.axis_index("col")
+    place = row % 4
+    core_row = row + 1 - 2 * (row % 2)
+    x_row = row + 2 - 4 * (place // 2)
+    core_place = place + 1 - 2 * (place % 2)
+    x_place = place + 2 - 4 * (place // 2)
+    diagonal_place = core_place + 2 - 4 * (core_place // 2)
+    places = (place, core_place, x_place, diagonal_place)
+    on_edge = (col % 3) == 0
+    inner = (col % 3) != 0
+    opposite = 3 - col
+    neighbour = col + 1 - 2 * (col % 2)
+    sum_partners = ((col + 2) % 4, opposite, neighbour)
+
+    def rows_of(k):
+        return pl.ds(pl.multiple_of(k * size, size), size)
+
+    def copy(kind, k):
+        at = rows_of(k)
+        source, target, device = {
+            EDGE_IN: (own_ref, zone.at[0], {"row": row, "col": neighbour}),
+            INNER_OWN: (own_ref, zone.at[1], {"row": row, "col": opposite}),
+            INNER_FORWARD: (zone.at[0], zone.at[2], {"row": row, "col": opposite}),
+            EDGE_OUT: (picked, zone.at[0], {"row": row, "col": neighbour}),
+            TO_CORE: (blocks.at[0], blocks.at[1], {"row": core_row, "col": col}),
+            TO_X: (blocks.at[0], blocks.at[2], {"row": x_row, "col": col}),
+            DIAGONAL: (blocks.at[2], blocks.at[3], {"row": core_row, "col": col}),
+        }[kind]
+        return pltpu.make_async_remote_copy(
+            src_ref=source.at[at, :], dst_ref=target.at[at, :],
+            send_sem=send_sem.at[kind, k], recv_sem=recv_sem.at[kind, k],
+            device_id=device, device_id_type=pl.DeviceIdType.MESH)
+
+    def q_copy(k, s):
+        slot = (k % 2) * 4 + s
+        start = pl.multiple_of(places[s] * piece + k * size, size)
+        return pltpu.make_async_copy(q_ref.at[:, pl.ds(start, size)], q_tiles.at[slot], q_sem.at[slot])
+
+    def sum_copy(i):
+        start = pl.multiple_of(sum_partners[i] * out_rows, out_rows)
+        return pltpu.make_async_remote_copy(
+            src_ref=acc.at[pl.ds(start, out_rows), :], dst_ref=parts.at[i],
+            send_sem=part_send.at[i], recv_sem=part_recv.at[i],
+            device_id={"row": row, "col": sum_partners[i]}, device_id_type=pl.DeviceIdType.MESH)
+
+    for k in range(2):
+        for s in range(4):
+            q_copy(k, s).start()
+
+    barrier = pltpu.get_barrier_semaphore()
+    for partner in sum_partners:
+        pl.semaphore_signal(barrier, inc=1, device_id={"row": row, "col": partner},
+                            device_id_type=pl.DeviceIdType.MESH)
+    for partner in (core_row, x_row):
+        pl.semaphore_signal(barrier, inc=1, device_id={"row": partner, "col": col},
+                            device_id_type=pl.DeviceIdType.MESH)
+    pl.semaphore_wait(barrier, 5)
+
+    def inner_issue(k):
+        copy(INNER_OWN, k).start()
+        copy(EDGE_IN, k).wait_recv()
+        copy(INNER_FORWARD, k).start()
+
+    @pl.when(on_edge)
+    def _():
+        @pl.loop(0, chunks)
+        def _(k):
+            copy(EDGE_IN, k).start()
+
+    @pl.when(inner)
+    def _():
+        inner_issue(0)
+        inner_issue(1)
+
+    acc[...] = jnp.zeros_like(acc)
+
+    def split(values):
+        high = values.astype(jnp.bfloat16)
+        low = (values - high.astype(jnp.float32)).astype(jnp.bfloat16)
+        return high, low
+
+    def right_side(k, s):
+        high, low = split(blocks[s, rows_of(k), :])
+        return jnp.concatenate([high, low, high], axis=0)
+
+    def add_product(k, s, right, start, height):
+        at = pl.ds(start, height)
+        high, low = split(q_tiles[(k % 2) * 4 + s, at, :])
+        left = jnp.concatenate([high, high, low], axis=1)
+        acc[at, :] += jnp.dot(left, right, preferred_element_type=jnp.float32)
+
+    @pl.loop(0, chunks + 1)
+    def _(k):
+        @pl.when(k < chunks)
+        def _():
+            at = rows_of(k)
+
+            @pl.when(inner)
+            def _():
+                @pl.when(k + 2 < chunks)
+                def _():
+                    inner_issue(k + 2)
+
+                copy(INNER_OWN, k).wait_recv()
+                copy(INNER_FORWARD, k).wait_recv()
+                own, third, fourth = own_ref[at, :], zone[1, at, :], zone[2, at, :]
+                for_edge = jnp.broadcast_to(sel_ref[1], own.shape)
+                picked[at, :] = jnp.where(for_edge == 2, third, jnp.where(for_edge == 3, fourth, own))
+                copy(EDGE_OUT, k).start()
+                mine = jnp.broadcast_to(sel_ref[0], own.shape)
+                near = jnp.where(mine == 0, own, zone[0, at, :])
+                blocks[0, at, :] = jnp.where(mine == 2, third, jnp.where(mine == 3, fourth, near))
+
+            @pl.when(on_edge)
+            def _():
+                copy(EDGE_OUT, k).wait_recv()
+                mine = jnp.broadcast_to(sel_ref[0], (size, cols))
+                blocks[0, at, :] = jnp.where(mine == 0, own_ref[at, :], zone[0, at, :])
+
+            copy(TO_X, k).start()
+            copy(TO_CORE, k).start()
+
+        @pl.when(k >= 1)
+        def _():
+            copy(TO_X, k - 1).wait_recv()
+            copy(DIAGONAL, k - 1).start()
+
+        @pl.when(k >= 2)
+        def _():
+            done = k - 2
+            copy(TO_CORE, done).wait_recv()
+            copy(DIAGONAL, done).wait_recv()
+            for s in range(4):
+                q_copy(done, s).wait()
+                right = right_side(done, s)
+
+                @pl.loop(0, piece // out_rows)
+                def _(r):
+                    add_product(done, s, right, pl.multiple_of(r * out_rows, out_rows), out_rows)
+
+                @pl.when(done + 2 < chunks)
+                def _():
+                    q_copy(done + 2, s).start()
+
+    last = chunks - 1
+    copy(TO_CORE, last).wait_recv()
+    copy(DIAGONAL, last).wait_recv()
+    for s in range(4):
+        q_copy(last, s).wait()
+    for i, target in enumerate(sum_partners + (col,)):
+        for s in range(4):
+            add_product(last, s, right_side(last, s), pl.multiple_of(target * out_rows, out_rows), out_rows)
+        if i < 3:
+            sum_copy(i).start()
+
+    total = acc[pl.ds(pl.multiple_of(col * out_rows, out_rows), out_rows), :]
+    for i in (2, 1, 0):
+        sum_copy(i).wait_recv()
+        total = total + parts[i]
+    out_ref[...] = total
+
+    for i in range(3):
+        sum_copy(i).wait_send()
+
+    @pl.loop(0, chunks)
+    def _(k):
+        @pl.when(on_edge)
+        def _():
+            copy(EDGE_IN, k).wait_send()
+
+        @pl.when(inner)
+        def _():
+            copy(INNER_OWN, k).wait_send()
+            copy(INNER_FORWARD, k).wait_send()
+            copy(EDGE_OUT, k).wait_send()
+
+        copy(TO_CORE, k).wait_send()
+        copy(TO_X, k).wait_send()
+        copy(DIAGONAL, k).wait_send()
+
+
+def merged_by_kernel(q_child, ordered, targets, col_index):
+    piece, cols = ordered.shape
+    chunks = CHUNKS
+    size = piece // chunks
+    places = jnp.arange(targets.shape[0], dtype=jnp.int32)
+    order = jnp.sum(jnp.where(targets[None, :] == places[:, None], places[None, :], 0), axis=1)
+    neighbour = col_index + 1 - 2 * (col_index % 2)
+    opposite = 3 - col_index
+    inner = (col_index % 3) != 0
+
+    def slot(source):
+        far = jnp.where(source == opposite, 2, 3)
+        return jnp.where(source == col_index, 0, jnp.where((source == neighbour) | ~inner, 1, far))
+
+    sel = jnp.stack([slot(order[col_index]), slot(order[neighbour])]).astype(jnp.int32)
+    out_rows = q_child.shape[0] // 4
+    return pl.pallas_call(
+        functools.partial(merge_kernel, chunks),
+        out_shape=jax.ShapeDtypeStruct((out_rows, cols), jnp.float32),
+        in_specs=[pl.BlockSpec(memory_space=pltpu.SMEM), pl.BlockSpec(memory_space=pltpu.VMEM),
+                  pl.BlockSpec(memory_space=pl.ANY)],
+        out_specs=pl.BlockSpec(memory_space=pltpu.VMEM),
+        scratch_shapes=[
+            pltpu.VMEM((3, piece, cols), jnp.float32),
+            pltpu.VMEM((piece, cols), jnp.float32),
+            pltpu.VMEM((4, piece, cols), jnp.float32),
+            pltpu.VMEM((q_child.shape[0], cols), jnp.float32),
+            pltpu.VMEM((3, out_rows, cols), jnp.float32),
+            pltpu.VMEM((8, q_child.shape[0], size), jnp.float32),
+            pltpu.SemaphoreType.DMA((7, chunks)),
+            pltpu.SemaphoreType.DMA((7, chunks)),
+            pltpu.SemaphoreType.DMA((3,)),
+            pltpu.SemaphoreType.DMA((3,)),
+            pltpu.SemaphoreType.DMA((8,)),
+        ],
+        compiler_params=pltpu.CompilerParams(
+            collective_id=0, has_side_effects=True, vmem_limit_bytes=56 * 1024 * 1024),
+        cost_estimate=pl.CostEstimate(
+            flops=6 * q_child.shape[0] * q_child.shape[1] * cols,
+            bytes_accessed=4 * q_child.shape[0] * q_child.shape[1], transcendentals=0),
+    )(sel, ordered, q_child)
+
+
+def merged_by_rings(q_child, ordered, targets, col_index):
     piece_rows = ordered.shape[0]
     row_count = lax.axis_size("row")
     col_count = lax.axis_size("col")
     half_count = row_count // 2
-    row_index = lax.axis_index("row")
-    col_index = lax.axis_index("col")
-    child_half = row_index // half_count
-    place_in_half = row_index % half_count
-    targets = lax.dynamic_index_in_dim(owner_order, child_half, 0, keepdims=False)
+    place_in_half = lax.axis_index("row") % half_count
 
     def advance(shifts, carry):
         travel, holding = carry
@@ -58,17 +285,26 @@
         return (going_up, going_down, block)
 
     _, _, secular_block = lax.fori_loop(1, half_count, collect_step, (holding, holding, own_block))
-    return lax.psum_scatter(
-        jnp.dot(
-            q_child,
-            secular_block,
-            precision=lax.Precision.HIGHEST,
-            preferred_element_type=jnp.float32,
-        ),
-        "col",
-        scatter_dimension=0,
-        tiled=True,
-    )
+    product = jnp.dot(q_child, secular_block, precision=lax.Precision.HIGHEST,
+                      preferred_element_type=jnp.float32)
+    return lax.psum_scatter(product, "col", scatter_dimension=0, tiled=True)
+
+
+def per_device(q_child, sec_weights, deflated, local_perm, owner_order):
+    kept_rows = (1 - deflated).astype(jnp.float32)[:, None]
+    masked = sec_weights * kept_rows
+    col_total = lax.psum(jnp.sum(masked * masked, axis=0), ("row", "col"))
+    row_count = lax.axis_size("row")
+    col_count = lax.axis_size("col")
+    child_half = lax.axis_index("row") // (row_count // 2)
+    targets = lax.dynamic_index_in_dim(owner_order, child_half, 0, keepdims=False)
+    ordered = jnp.take(masked, local_perm[0], axis=0)
+    col_index = lax.axis_index("col")
+    piece = ordered.shape[0]
+    fits = row_count == 8 and col_count == 4 and piece % (CHUNKS * 128) == 0
+    merge = merged_by_kernel if fits else merged_by_rings
+    merged = merge(q_child, ordered, targets, col_index)
+    return merged * lax.rsqrt(col_total + 1e-06)[None, :]
 
 
 def solution(mesh):

time: 571 us -> 222 us (0.39)
  waiting for transfers between devices: 235 us -> 0 us
  Pallas kernels: 0 us -> 152 us
  matrix products: 112 us -> 0 us
  starting transfers between devices: 93.5 us -> 0 us
  local copies, waits for them, and re-layouts: 55.3 us -> 9.84 us
  between operations: 14 us -> 3.71 us
  other arithmetic: 16.4 us -> 8.55 us
    pallas_call x0 -> x1, Pallas kernels: none -> 152 us  [merged_by_kernel(): pl.pallas_call(functools.partial(merge_kernel, chunks), out_shape=jax.Sha...]
    ppermute x9 -> x0, waiting for transfers between devices: 149 us -> none  [the longest x3 137 us: passed_along(): lax.ppermute(array, axis, [(i, (i + by) % length) for i in range(length)])]
    dot_general x1 -> x0, matrix products: 112 us -> none  [per_device(): jnp.dot(q_child, secular_block, precision=lax.Precision.HIGHEST, preferre...]
    ppermute x9 -> x0, starting transfers between devices: 93.5 us -> none  [the longest x6 92 us: shifted(): return lax.ppermute(array, axis, pairs)]
    reduce_scatter x1 -> x0, waiting for transfers between devices: 86.4 us -> none  [per_device(): lax.psum_scatter(jnp.dot(q_child, secular_block, precision=lax.Precision....]
    while x33 -> x0, local copies, waits for them, and re-layouts: 32.8 us -> none
    select_n x11 -> x2, other arithmetic: 11.8 us -> 3.29 us  [per_device(): ordered = jnp.take(masked, local_perm[0], axis=0)]
    unnamed x7 -> x4, local copies, waits for them, and re-layouts: 7.33 us -> 0.68 us
  transfers between devices with their start and end apart: 10 -> 0, of which waited for: 10 -> 0; matrix products, arithmetic and copies ran while one was open for 1% -> 0% of each run, Pallas kernels for 0% -> 0%
where the time goes in v1:
time: 222 us
  Pallas kernels  152 us (68%)
  blocking collectives  47.1 us (21%)
  local copies, waits for them, and re-layouts  9.84 us (4%)
  other arithmetic  8.55 us (4%)
  between operations  3.71 us (2%)
    pallas_call x1, Pallas kernels, merged_by_kernel(): pl.pallas_call(functools.partial(merge_kernel, chunks), out_shape=jax.Sha...  152 us
    psum x1, blocking collectives, per_device(): col_total = lax.psum(jnp.sum(masked * masked, axis=0), ('row', 'col'))  47.1 us
    gather x1, local copies, waits for them, and re-layouts, per_device(): ordered = jnp.take(masked, local_perm[0], axis=0)  8.56 us

profile of v1, /device:TPU:0, one launch (start us, length us, event | category | flops | bytes accessed | tf_op | source)
XLA Modules:
  0.0 221.5 jit_solution(10690078478042725380)
XLA Ops:
  0.0 0.0 copy-start
  0.0 0.7 copy-done
  0.7 0.1 select_reduce_fusion
  0.8 0.6 fusion
  5.1 0.6 pad_add_fusion.sel_ref
  5.7 0.7 subtract_convert_fusion
  6.4 0.0 copy-start.1
  6.4 2.0 multiply_reduce_fusion
  8.3 0.0 copy-done.1
  8.4 8.6 %gather_fusion = f32[2048,256]{1,0:T(8,128)} fusion(f32[2048,256]{1,0:T(8,128)S(1)} %get-tuple-element.6, s32[2048]{0:T(1024)S(1)} %broadcast_clamp_fusion), kind=kCustom, calls=%fused_computation | custom fusion | bytes 4202496 | tf_op jit(solution)/shard_map/jit(_take)/gather | solution.py:301
  16.9 3.3 %broadcast_select_fusion.own_ref = f32[2048,256]{1,0:T(8,128)} fusion(f32[2048,256]{1,0:T(8,128)} %gather_fusion, pred[2048]{0:T(1024)(128)(4,1)S(1)} %compare_and_fusion), kind=kLoop, calls=%fused_computation.2 | loop fusion | flops 524288 | bytes 4196352 | tf_op jit(solution)/shard_map/jit(_take)/select_n | solution.py:301
  20.2 152.4 %shard_map.55 = f32[512,256]{1,0:T(8,128)} custom-call(s32[2]{0:T(128)} %pad_add_fusion.sel_ref, f32[2048,256]{1,0:T(8,128)} %broadcast_select_fusion.own_ref, f32[2048,8192]{1,0:T(8,128)} %q_ref.1), custom_call_target="tpu_custom_call" | custom-call | flops 25769803776 | bytes 67108864 | tf_op jit(solution)/shard_map/pallas_call | solution.py:227
  172.6 47.1 %psum.7 = f32[256]{0:T(256)S(1)} all-reduce(f32[256]{0:T(256)S(1)} %get-tuple-element.5), channel_id=1, replica_groups=mesh['row'=8,'col'=4] {'row','col'}, use_global_device_ids=true, to_apply=%region_2.3 | all-reduce | flops 256 | bytes 2048 | tf_op jit(solution)/shard_map/psum | solution.py:296
  219.7 1.9 broadcast_multiply_fusion.1
  (5 shorter events, 0.0 us)
Async XLA Ops:
  0.0 0.7 copy-start
  6.4 2.0 copy-start.1

commit v2 on v1

--- a/solution.py
+++ b/solution.py
@@ -21,11 +21,12 @@
     return lax.ppermute(array, axis, pairs)
 
 
-def merge_kernel(chunks, sel_ref, own_ref, q_ref, out_ref, zone, picked, blocks, acc, parts, q_tiles,
-                 send_sem, recv_sem, part_send, part_recv, q_sem):
+def merge_kernel(chunks, one_crosses, owner_ref, own_ref, squares_ref, q_ref, out_ref, zone, picked, blocks, acc,
+                 parts, q_tiles, sums, sums_in, send_sem, recv_sem, part_send, part_recv, sums_send, sums_recv, q_sem):
     piece, cols = own_ref.shape
     size = piece // chunks
     out_rows = out_ref.shape[0]
+    ahead = 1 if one_crosses else 2
     row = lax.axis_index("row")
     col = lax.axis_index("col")
     place = row % 4
@@ -39,7 +40,25 @@
     inner = (col % 3) != 0
     opposite = 3 - col
     neighbour = col + 1 - 2 * (col % 2)
-    sum_partners = ((col + 2) % 4, opposite, neighbour)
+    skew = (col + 2) % 4
+    y_row = row + 4 - 8 * (row // 4)
+    child = row // 4
+    partners = tuple({"row": r, "col": col} for r in (core_row, x_row, y_row)) + tuple(
+        {"row": row, "col": c} for c in (neighbour, opposite))
+
+    def slot_of(target):
+        source = 0
+        for j in range(4):
+            source = source + jnp.where(owner_ref[child, j] == target, j, 0)
+        far = jnp.where(source == opposite, 2, 3)
+        far = jnp.where(source == neighbour, 1, far)
+        return jnp.where(source == col, 0, far)
+
+    my_slot = slot_of(col)
+    edge_slot = slot_of(neighbour)
+    near_target = owner_ref[child, neighbour]
+    low_side = jnp.where(col < 2, 1, 0)
+    edge_crosses = jnp.where(near_target < 2, 1 - low_side, low_side)
 
     def rows_of(k):
         return pl.ds(pl.multiple_of(k * size, size), size)
@@ -48,7 +67,7 @@
         at = rows_of(k)
         source, target, device = {
             EDGE_IN: (own_ref, zone.at[0], {"row": row, "col": neighbour}),
-            INNER_OWN: (own_ref, zone.at[1], {"row": row, "col": opposite}),
+            INNER_OWN: (zone.at[2] if one_crosses else own_ref, zone.at[1], {"row": row, "col": opposite}),
             INNER_FORWARD: (zone.at[0], zone.at[2], {"row": row, "col": opposite}),
             EDGE_OUT: (picked, zone.at[0], {"row": row, "col": neighbour}),
             TO_CORE: (blocks.at[0], blocks.at[1], {"row": core_row, "col": col}),
@@ -65,30 +84,42 @@
         start = pl.multiple_of(places[s] * piece + k * size, size)
         return pltpu.make_async_copy(q_ref.at[:, pl.ds(start, size)], q_tiles.at[slot], q_sem.at[slot])
 
-    def sum_copy(i):
-        start = pl.multiple_of(sum_partners[i] * out_rows, out_rows)
+    def part_rows(target):
+        return pl.ds(pl.multiple_of(target * out_rows, out_rows), out_rows)
+
+    def part_copy(i):
+        target, device = ((skew, neighbour), (neighbour, neighbour), (opposite, opposite))[i]
         return pltpu.make_async_remote_copy(
-            src_ref=acc.at[pl.ds(start, out_rows), :], dst_ref=parts.at[i],
+            src_ref=acc.at[part_rows(target), :], dst_ref=parts.at[i],
             send_sem=part_send.at[i], recv_sem=part_recv.at[i],
-            device_id={"row": row, "col": sum_partners[i]}, device_id_type=pl.DeviceIdType.MESH)
+            device_id={"row": row, "col": device}, device_id_type=pl.DeviceIdType.MESH)
+
+    def sums_copy(i):
+        return pltpu.make_async_remote_copy(
+            src_ref=sums.at[i], dst_ref=sums_in.at[i], send_sem=sums_send.at[i], recv_sem=sums_recv.at[i],
+            device_id=partners[i], device_id_type=pl.DeviceIdType.MESH)
 
     for k in range(2):
         for s in range(4):
             q_copy(k, s).start()
 
     barrier = pltpu.get_barrier_semaphore()
-    for partner in sum_partners:
-        pl.semaphore_signal(barrier, inc=1, device_id={"row": row, "col": partner},
-                            device_id_type=pl.DeviceIdType.MESH)
-    for partner in (core_row, x_row):
-        pl.semaphore_signal(barrier, inc=1, device_id={"row": partner, "col": col},
-                            device_id_type=pl.DeviceIdType.MESH)
+    for partner in partners:
+        pl.semaphore_signal(barrier, inc=1, device_id=partner, device_id_type=pl.DeviceIdType.MESH)
+    sums[0] = jnp.broadcast_to(squares_ref[...], sums.shape[1:])
     pl.semaphore_wait(barrier, 5)
 
     def inner_issue(k):
-        copy(INNER_OWN, k).start()
-        copy(EDGE_IN, k).wait_recv()
-        copy(INNER_FORWARD, k).start()
+        if one_crosses:
+            at = rows_of(k)
+            copy(EDGE_IN, k).wait_recv()
+            crossing = jnp.broadcast_to(edge_crosses, (size, cols))
+            zone[2, at, :] = jnp.where(crossing == 1, zone[0, at, :], own_ref[at, :])
+            copy(INNER_OWN, k).start()
+        else:
+            copy(INNER_OWN, k).start()
+            copy(EDGE_IN, k).wait_recv()
+            copy(INNER_FORWARD, k).start()
 
     @pl.when(on_edge)
     def _():
@@ -98,9 +129,10 @@
 
     @pl.when(inner)
     def _():
-        inner_issue(0)
-        inner_issue(1)
-
+        for k in range(ahead):
+            inner_issue(k)
+
+    sums_copy(0).start()
     acc[...] = jnp.zeros_like(acc)
 
     def split(values):
@@ -120,30 +152,41 @@
 
     @pl.loop(0, chunks + 1)
     def _(k):
+        for i in range(4):
+            @pl.when(k == i + 1)
+            def _():
+                sums_copy(i).wait_recv()
+                sums[i + 1] = sums[i] + sums_in[i]
+                sums_copy(i + 1).start()
+
         @pl.when(k < chunks)
         def _():
             at = rows_of(k)
 
             @pl.when(inner)
             def _():
-                @pl.when(k + 2 < chunks)
+                @pl.when(k + ahead < chunks)
                 def _():
-                    inner_issue(k + 2)
+                    inner_issue(k + ahead)
 
                 copy(INNER_OWN, k).wait_recv()
-                copy(INNER_FORWARD, k).wait_recv()
-                own, third, fourth = own_ref[at, :], zone[1, at, :], zone[2, at, :]
-                for_edge = jnp.broadcast_to(sel_ref[1], own.shape)
+                own, third = own_ref[at, :], zone[1, at, :]
+                if one_crosses:
+                    fourth = third
+                else:
+                    copy(INNER_FORWARD, k).wait_recv()
+                    fourth = zone[2, at, :]
+                for_edge = jnp.broadcast_to(edge_slot, own.shape)
                 picked[at, :] = jnp.where(for_edge == 2, third, jnp.where(for_edge == 3, fourth, own))
                 copy(EDGE_OUT, k).start()
-                mine = jnp.broadcast_to(sel_ref[0], own.shape)
+                mine = jnp.broadcast_to(my_slot, own.shape)
                 near = jnp.where(mine == 0, own, zone[0, at, :])
                 blocks[0, at, :] = jnp.where(mine == 2, third, jnp.where(mine == 3, fourth, near))
 
             @pl.when(on_edge)
             def _():
                 copy(EDGE_OUT, k).wait_recv()
-                mine = jnp.broadcast_to(sel_ref[0], (size, cols))
+                mine = jnp.broadcast_to(my_slot, (size, cols))
                 blocks[0, at, :] = jnp.where(mine == 0, own_ref[at, :], zone[0, at, :])
 
             copy(TO_X, k).start()
@@ -176,20 +219,30 @@
     copy(DIAGONAL, last).wait_recv()
     for s in range(4):
         q_copy(last, s).wait()
-    for i, target in enumerate(sum_partners + (col,)):
+
+    def finish(target):
         for s in range(4):
             add_product(last, s, right_side(last, s), pl.multiple_of(target * out_rows, out_rows), out_rows)
-        if i < 3:
-            sum_copy(i).start()
-
-    total = acc[pl.ds(pl.multiple_of(col * out_rows, out_rows), out_rows), :]
-    for i in (2, 1, 0):
-        sum_copy(i).wait_recv()
-        total = total + parts[i]
-    out_ref[...] = total
+
+    finish(skew)
+    part_copy(0).start()
+    finish(opposite)
+    finish(neighbour)
+    part_copy(0).wait_recv()
+    acc[part_rows(opposite), :] += parts[0]
+    part_copy(2).start()
+    part_copy(1).start()
+    finish(col)
+    sums_copy(4).wait_recv()
+    scale = lax.rsqrt(sums[4] + sums_in[4] + 1e-06)[0:1, :]
+    part_copy(1).wait_recv()
+    part_copy(2).wait_recv()
+    out_ref[...] = (acc[part_rows(col), :] + parts[1] + parts[2]) * scale
 
     for i in range(3):
-        sum_copy(i).wait_send()
+        part_copy(i).wait_send()
+    for i in range(5):
+        sums_copy(i).wait_send()
 
     @pl.loop(0, chunks)
     def _(k):
@@ -200,7 +253,8 @@
         @pl.when(inner)
         def _():
             copy(INNER_OWN, k).wait_send()
-            copy(INNER_FORWARD, k).wait_send()
+            if not one_crosses:
+                copy(INNER_FORWARD, k).wait_send()
             copy(EDGE_OUT, k).wait_send()
 
         copy(TO_CORE, k).wait_send()
@@ -208,27 +262,16 @@
         copy(DIAGONAL, k).wait_send()
 
 
-def merged_by_kernel(q_child, ordered, targets, col_index):
+def merged_by_kernel(one_crosses, owner_order, ordered, squares, q_child):
     piece, cols = ordered.shape
     chunks = CHUNKS
     size = piece // chunks
-    places = jnp.arange(targets.shape[0], dtype=jnp.int32)
-    order = jnp.sum(jnp.where(targets[None, :] == places[:, None], places[None, :], 0), axis=1)
-    neighbour = col_index + 1 - 2 * (col_index % 2)
-    opposite = 3 - col_index
-    inner = (col_index % 3) != 0
-
-    def slot(source):
-        far = jnp.where(source == opposite, 2, 3)
-        return jnp.where(source == col_index, 0, jnp.where((source == neighbour) | ~inner, 1, far))
-
-    sel = jnp.stack([slot(order[col_index]), slot(order[neighbour])]).astype(jnp.int32)
     out_rows = q_child.shape[0] // 4
     return pl.pallas_call(
-        functools.partial(merge_kernel, chunks),
+        functools.partial(merge_kernel, chunks, one_crosses),
         out_shape=jax.ShapeDtypeStruct((out_rows, cols), jnp.float32),
         in_specs=[pl.BlockSpec(memory_space=pltpu.SMEM), pl.BlockSpec(memory_space=pltpu.VMEM),
-                  pl.BlockSpec(memory_space=pl.ANY)],
+                  pl.BlockSpec(memory_space=pltpu.VMEM), pl.BlockSpec(memory_space=pl.ANY)],
         out_specs=pl.BlockSpec(memory_space=pltpu.VMEM),
         scratch_shapes=[
             pltpu.VMEM((3, piece, cols), jnp.float32),
@@ -237,18 +280,22 @@
             pltpu.VMEM((q_child.shape[0], cols), jnp.float32),
             pltpu.VMEM((3, out_rows, cols), jnp.float32),
             pltpu.VMEM((8, q_child.shape[0], size), jnp.float32),
+            pltpu.VMEM((5, 8, cols), jnp.float32),
+            pltpu.VMEM((5, 8, cols), jnp.float32),
             pltpu.SemaphoreType.DMA((7, chunks)),
             pltpu.SemaphoreType.DMA((7, chunks)),
             pltpu.SemaphoreType.DMA((3,)),
             pltpu.SemaphoreType.DMA((3,)),
+            pltpu.SemaphoreType.DMA((5,)),
+            pltpu.SemaphoreType.DMA((5,)),
             pltpu.SemaphoreType.DMA((8,)),
         ],
         compiler_params=pltpu.CompilerParams(
-            collective_id=0, has_side_effects=True, vmem_limit_bytes=56 * 1024 * 1024),
+            collective_id=1 if one_crosses else 2, has_side_effects=True, vmem_limit_bytes=56 * 1024 * 1024),
         cost_estimate=pl.CostEstimate(
             flops=6 * q_child.shape[0] * q_child.shape[1] * cols,
             bytes_accessed=4 * q_child.shape[0] * q_child.shape[1], transcendentals=0),
-    )(sel, ordered, q_child)
+    )(owner_order, ordered, squares, q_child)
 
 
 def merged_by_rings(q_child, ordered, targets, col_index):
@@ -293,17 +340,22 @@
 def per_device(q_child, sec_weights, deflated, local_perm, owner_order):
     kept_rows = (1 - deflated).astype(jnp.float32)[:, None]
     masked = sec_weights * kept_rows
-    col_total = lax.psum(jnp.sum(masked * masked, axis=0), ("row", "col"))
+    squares = jnp.sum(masked * masked, axis=0)
     row_count = lax.axis_size("row")
     col_count = lax.axis_size("col")
+    ordered = masked.at[local_perm[0]].get(mode="promise_in_bounds", unique_indices=True)
+    piece = ordered.shape[0]
+    if row_count == 8 and col_count == 4 and piece % (CHUNKS * 128) == 0:
+        crossing = jnp.sum((owner_order[:, :2] >= 2).astype(jnp.int32), axis=1)
+        return lax.cond(
+            jnp.max(crossing) <= 1,
+            functools.partial(merged_by_kernel, True),
+            functools.partial(merged_by_kernel, False),
+            owner_order, ordered, squares[None, :], q_child)
+    col_total = lax.psum(squares, ("row", "col"))
     child_half = lax.axis_index("row") // (row_count // 2)
     targets = lax.dynamic_index_in_dim(owner_order, child_half, 0, keepdims=False)
-    ordered = jnp.take(masked, local_perm[0], axis=0)
-    col_index = lax.axis_index("col")
-    piece = ordered.shape[0]
-    fits = row_count == 8 and col_count == 4 and piece % (CHUNKS * 128) == 0
-    merge = merged_by_kernel if fits else merged_by_rings
-    merged = merge(q_child, ordered, targets, col_index)
+    merged = merged_by_rings(q_child, ordered, targets, lax.axis_index("col"))
     return merged * lax.rsqrt(col_total + 1e-06)[None, :]
 
 

time: 222 us -> 143 us (0.64)
  blocking collectives: 47.1 us -> 0 us
  Pallas kernels: 152 us -> 127 us
  other arithmetic: 8.55 us -> 4.95 us
  between operations: 3.71 us -> 0.69 us
    psum x1 -> x0, blocking collectives: 47.1 us -> none  [per_device(): col_total = lax.psum(jnp.sum(masked * masked, axis=0), ('row', 'col'))]
    pallas_call x1, Pallas kernels: 152 us -> 127 us  [merged_by_kernel(): pl.pallas_call(functools.partial(merge_kernel, chunks, one_crosses), out_...]
    select_n x2 -> x1, other arithmetic: 3.29 us -> 0.01 us  [per_device(): masked.at[local_perm[0]].get(mode='promise_in_bounds', unique_indices=True)]
where the time goes in v2:
time: 143 us; the launch traced here: 142 us
  Pallas kernels  127 us (89%)
  local copies, waits for them, and re-layouts  9.37 us (7%)
  other arithmetic  4.95 us (3%)
    pallas_call x1, Pallas kernels, merged_by_kernel(): pl.pallas_call(functools.partial(merge_kernel, chunks, one_crosses), out_...  127 us
    gather x1, local copies, waits for them, and re-layouts, per_device(): masked.at[local_perm[0]].get(mode='promise_in_bounds', unique_indices=True)  8.56 us

profile of v2, /device:TPU:0, one launch (start us, length us, event | category | flops | bytes accessed | tf_op | source)
XLA Modules:
  0.0 142.4 jit_solution(9811559574561876927)
XLA Ops:
  0.0 0.8 fusion
  0.8 0.6 reduce_max.9
  2.1 0.7 subtract_convert_fusion
  2.8 0.0 copy-start
  2.8 0.0 copy-start.1
  2.8 2.0 %broadcast_multiply_fusion = f32[2048,256]{1,0:T(8,128)S(1)} fusion(f32[2048,256]{1,0:T(8,128)} %param.8, f32[2048]{0:T(1024)S(1)} %subtract_convert_fusion), kind=kLoop, calls=%fused_computation.8 | loop fusion | flops 524288 | bytes 4202496 | tf_op jit(solution)/shard_map/mul | solution.py:342
  4.8 0.0 copy-done
  4.8 0.0 copy-done.1
  4.8 136.8 %conditional.1 = (f32[512,256]{1,0:T(8,128)S(1)}) conditional(s32[]{:T(128)} %convert_element_type.10, (s32[2,4]{1,0:T(2,128)S(1)}, f32[2048,256]{1,0:T(8,128)S(1)}, f32[2048,256]{1,0:T(8,128)S(1)}, f32[2048,8192]{1,0:T(8,128)}, s32[2048,1]{0,1:T(1,128)S(1)}, /*index=5*/s32[2048,1]{0,1:T(1,128)S(1)}, s32[2048,1]{0,1:T(1,128)S(1)}, ...), branch_computations={%region_3.0_spmd.clone, %region_4.0_spmd.clone} | conditional | flops 25770860544 | bytes 73458696 | solution.py:350
  4.8 0.9 multiply_reduce_fusion.1
  5.7 8.6 %gather_fusion.1 = f32[2048,256]{1,0:T(8,128)} fusion(f32[2048,256]{1,0:T(8,128)S(1)} %get-tuple-element.89, s32[2048]{0:T(1024)S(1)} %broadcast_clamp_fusion.1), kind=kCustom, calls=%fused_computation.1 | custom fusion | bytes 4202496 | tf_op jit(solution)/shard_map/gather | solution.py:346
  14.2 127.1 %branch_1_fun.1 = f32[512,256]{1,0:T(8,128)S(1)} custom-call(s32[2,4]{1,0:T(2,128)S(1)} %get-tuple-element.83.owner_ref, f32[2048,256]{1,0:T(8,128)} %gather_fusion.1, f32[1,256]{1,0:T(1,128)} %bitcast.14, f32[2048,8192]{1,0:T(8,128)} %get-tuple-element.86.q_ref), custom_call_target="tpu_custom_call" | custom-call | flops 25769803776 | bytes 67108864 | tf_op jit(solution)/shard_map/cond/branch_1_fun/pallas_call | solution.py:270
  141.6 0.8 copy.17
  (2 shorter events, 0.0 us)
Async XLA Ops:
  2.8 2.0 %copy-start = (s32[1,2048]{1,0:T(1,128)S(1)}, s32[1,2048]{1,0:T(1,128)}, u32[]{:S(2)}) copy-start(s32[1,2048]{1,0:T(1,128)} %param.10) | copy-start | bytes 24580
  2.8 2.0 %copy-start.1 = (s32[2,4]{1,0:T(2,128)S(1)}, s32[2,4]{1,0:T(2,128)}, u32[]{:S(2)}) copy-start(s32[2,4]{1,0:T(2,128)} %param.11) | copy-start | bytes 100
